TPU v7x, 32 devices: a whole 2x2x4 slice. The times are simulated.
32 devices in a mesh: dp: 8 (over y, x, core), mp: 4 (over z).
Axes of the slice: x: 2, y: 2, z: 4, core: 2. Of those that a mesh axis runs over, the one named last changes fastest.
Arguments:
- hidden: bfloat16 [128, 1024], P('dp'), may hold values from -6 to 6
- attn_gain: float32 [1024], replicated, may hold values from 0.25 to 1.75
- w_qkv: bfloat16 [1024, 3, 1024], P(None, None, 'mp'), may hold values from -2 to 2
- w_out: bfloat16 [1024, 1024], P('mp'), may hold values from -0.1875 to 0.1875
- mlp_gain: float32 [1024], replicated, may hold values from 0.25 to 1.75
- w_gate_up: bfloat16 [1024, 2, 4096], P(None, None, 'mp'), may hold values from -0.1875 to 0.1875
- w_down: bfloat16 [4096, 1024], P('mp'), may hold values from -0.09375 to 0.09375
- kv_cache: bfloat16 [2, 1024, 128, 1024], P(None, 'dp', None, 'mp'), may hold values from -9 to 9
- lengths: int32 [128], replicated, may hold values from 1 to 16384, as said below
- page_request: int32 [1024], P('dp'), may hold values from -1 to 127, as said below
- page_index: int32 [1024], P('dp'), may hold values from 0 to 127, as said below
Outputs:
- appended: bfloat16 [2, 128, 1024], P(None, 'dp', 'mp')
- hidden_out: bfloat16 [128, 1024], P('dp')
Inputs may be any that keep to these rules, and one draw needn't show every extreme that they name: `lengths`: 1 request hold exactly 16384 tokens, the others fewer than 512. `page_request`: each request owns exactly ceil(lengths / 128) pool pages, which may lie on any data devices; -1 marks an empty page. `page_index`: the pages of a request carry the places 0 to ceil(lengths / 128) - 1, each once; empty pages carry 0.
All inputs are finite; a program needn't handle non-finite values.
Results may differ from a plain program's by a relative error of at most 0.0085.
Values may be sent and summed in bfloat16 or wider, within the bound.
A program may use at most 128 MiB of HBM per device.

v0:
```python
import jax
import jax.numpy as jnp
from jax import lax
from jax.sharding import PartitionSpec as P

HEAD_DIM = 64
PAGE_BLOCK = 8


EPSILON = 1e-05
NEGATIVE = -1e30


def merged_2(value, axis, join):
    pieces = jax.tree.map(lambda part: lax.all_gather(part, axis), value)
    head = jax.tree.map(lambda part: part[0], pieces)
    tail = jax.tree.map(lambda part: part[1:], pieces)
    running, _ = lax.scan(lambda running, piece: (join(running, piece), None), head, tail)
    return running


def rms_norm(values, gain):
    widened = values.astype(jnp.float32)
    mean_square = jnp.mean(widened * widened, axis=-1, keepdims=True)
    return (widened * lax.rsqrt(mean_square + EPSILON) * gain).astype(jnp.bfloat16)


def combine(first, second):
    largest = jnp.maximum(first[0], second[0])
    shrink_first = jnp.exp(first[0] - largest)
    shrink_second = jnp.exp(second[0] - largest)
    totals = first[1] * shrink_first + second[1] * shrink_second
    weighted = first[2] * shrink_first[:, :, None] + second[2] * shrink_second[:, :, None]
    return (largest, totals, weighted)


def body(
    hidden,
    attn_gain,
    w_qkv,
    w_out,
    mlp_gain,
    w_gate_up,
    w_down,
    kv_cache,
    lengths,
    page_request,
    page_index,
):
    local_rows = hidden.shape[0]
    head_cols = w_qkv.shape[2]
    local_heads = head_cols // HEAD_DIM
    pool_pages = kv_cache.shape[1]
    page_len = kv_cache.shape[2]
    data_devices = lax.axis_size("dp")
    requests = local_rows * data_devices
    score_scale = HEAD_DIM ** (-0.5)
    normed = rms_norm(hidden, attn_gain)
    projected = jnp.dot(
        normed, w_qkv.reshape(w_qkv.shape[0], 3 * head_cols), preferred_element_type=jnp.float32
    )
    projected = lax.optimization_barrier(projected.astype(jnp.bfloat16)).reshape(
        local_rows, 3, head_cols
    )
    appended = jnp.stack([projected[:, 1], projected[:, 2]])
    every_query = lax.all_gather(projected[:, 0], "dp", axis=0, tiled=True)
    own_queries = projected[:, 0].reshape(local_rows, local_heads, HEAD_DIM).astype(jnp.float32)
    own_keys = projected[:, 1].reshape(local_rows, local_heads, HEAD_DIM).astype(jnp.float32)
    own_values = projected[:, 2].reshape(local_rows, local_heads, HEAD_DIM).astype(jnp.float32)
    self_scores = jnp.sum(own_queries * own_keys, axis=-1) * score_scale
    home_row = lax.axis_index("dp") * local_rows
    start_max = lax.dynamic_update_slice(
        jnp.full((requests, local_heads), NEGATIVE, jnp.float32), self_scores, (home_row, 0)
    )
    start_totals = lax.dynamic_update_slice(
        jnp.zeros((requests, local_heads), jnp.float32),
        jnp.ones((local_rows, local_heads), jnp.float32),
        (home_row, 0),
    )
    start_weighted = lax.dynamic_update_slice(
        jnp.zeros((requests, local_heads, HEAD_DIM), jnp.float32), own_values, (home_row, 0, 0)
    )
    visit_order = jnp.arange(pool_pages, dtype=jnp.int32)
    trip_count = pool_pages // PAGE_BLOCK
    request_ids = jnp.arange(requests, dtype=jnp.int32)
    offsets = jnp.arange(page_len, dtype=jnp.int32)

    def visit(step_index, carry):
        running_max, totals, weighted = carry
        picked = lax.dynamic_slice_in_dim(visit_order, step_index * PAGE_BLOCK, PAGE_BLOCK, 0)
        fetched = jnp.take(kv_cache, picked, axis=1)
        owners = page_request[picked]
        page_pos = page_index[picked]
        clamped = jnp.maximum(owners, 0)
        chosen_queries = every_query[clamped].reshape(PAGE_BLOCK, local_heads, HEAD_DIM)
        key_rows = fetched[0].reshape(PAGE_BLOCK, page_len, local_heads, HEAD_DIM)
        value_rows = fetched[1].reshape(PAGE_BLOCK, page_len, local_heads, HEAD_DIM)
        scores = (
            jnp.einsum(
                "phd,pthd->pht", chosen_queries, key_rows, preferred_element_type=jnp.float32
            )
            * score_scale
        )
        position = page_pos[:, None] * page_len + offsets[None, :]
        usable = (owners[:, None] >= 0) & (position < lengths[clamped][:, None])
        page_max = jnp.max(jnp.where(usable[:, None, :], scores, NEGATIVE), axis=2)
        raw = jnp.where(usable[:, None, :], jnp.exp(scores - page_max[:, :, None]), 0.0)
        page_total = jnp.sum(raw, axis=2)
        page_sum = jnp.einsum(
            "pht,pthd->phd",
            raw.astype(jnp.bfloat16),
            value_rows,
            preferred_element_type=jnp.float32,
        )
        member = owners[:, None] == request_ids[None, :]
        candidate = jnp.max(jnp.where(member[:, :, None], page_max[:, None, :], NEGATIVE), axis=0)
        new_max = jnp.maximum(running_max, candidate)
        factors = jnp.where(owners[:, None] >= 0, jnp.exp(page_max - new_max[clamped]), 0.0)
        rescale = jnp.exp(running_max - new_max)
        onehot = member.astype(jnp.float32)
        totals = totals * rescale + jnp.einsum(
            "pr,ph->rh", onehot, page_total * factors, precision=lax.Precision.HIGHEST
        )
        weighted = weighted * rescale[:, :, None] + jnp.einsum(
            "pr,phd->rhd", onehot, page_sum * factors[:, :, None], precision=lax.Precision.HIGHEST
        )
        return (new_max, totals, weighted)

    running_max, totals, weighted = lax.fori_loop(
        0, trip_count, visit, (start_max, start_totals, start_weighted)
    )
    merged = merged_2((running_max, totals, weighted), "dp", combine)
    own_totals = lax.dynamic_slice_in_dim(merged[1], home_row, local_rows, 0)
    own_weighted = lax.dynamic_slice_in_dim(merged[2], home_row, local_rows, 0)
    context = (
        (own_weighted / own_totals[:, :, None]).reshape(local_rows, head_cols).astype(jnp.bfloat16)
    )
    attended = lax.psum(jnp.dot(context, w_out, preferred_element_type=jnp.float32), "mp")
    residual = lax.optimization_barrier(
        (hidden.astype(jnp.float32) + attended).astype(jnp.bfloat16)
    )
    normed_mlp = rms_norm(residual, mlp_gain)
    hidden_cols = w_gate_up.shape[2]
    gate_up = jnp.dot(
        normed_mlp,
        w_gate_up.reshape(w_gate_up.shape[0], 2 * hidden_cols),
        preferred_element_type=jnp.float32,
    ).reshape(local_rows, 2, hidden_cols)
    activated = (jax.nn.silu(gate_up[:, 0]) * gate_up[:, 1]).astype(jnp.bfloat16)
    lowered = lax.psum(jnp.dot(activated, w_down, preferred_element_type=jnp.float32), "mp")
    hidden_out = (residual.astype(jnp.float32) + lowered).astype(jnp.bfloat16)
    return (appended, hidden_out)


def solution(mesh):
    return jax.shard_map(
        body,
        mesh=mesh,
        in_specs=(
            P("dp", None),
            P(),
            P(None, None, "mp"),
            P("mp", None),
            P(),
            P(None, None, "mp"),
            P("mp", None),
            P(None, "dp", None, "mp"),
            P(),
            P("dp"),
            P("dp"),
        ),
        out_specs=(P(None, "dp", "mp"), P("dp", None)),
        check_vma=False,
    )
```

profile of v0, /device:TPU:0, one launch (start us, length us, event | category | flops | bytes accessed | tf_op | source)
XLA Modules:
  0.0 380.0 jit_solution(6839596897014683295)
XLA Ops:
  13.3 10.7 %all-gather = bf16[128,1,256]{2,0,1:T(8,128)(2,1)S(1)} all-gather(bf16[16,1,256]{2,0,1:T(8,128)(2,1)S(1)} %copy.113), channel_id=2, replica_groups=mesh['dp'=8,'mp'=4] {'dp'}, dimensions={0}, use_global_device_ids=true | all-gather | bytes 73728 | tf_op jit(solution)/shard_map/all_gather | solution.py:66
  24.8 230.0 %while.34 = (s32[]{:T(128)}, f32[128,4]{0,1:T(4,128)S(1)}, f32[128,4]{0,1:T(4,128)S(1)}, f32[128,4,64]{0,2,1:T(8,128)S(1)}, s32[128]{0:T(128)S(1)}, /*index=5*/s...) while((s32[]{:T(128)}, f32[128,4]{0,1:T(4,128)S(1)}, ...), condition=%wide.region_6.7_spmd.clone, body=%wide.region_2.6_spmd.clone.sunk | while | flops 4886126 | bytes 9842463 | solution.py:129
  27.6 6.4 %gather_fusion.2 = bf16[8,2,128,256]{3,2,1,0:T(8,128)(2,1)S(1)} fusion(bf16[2,128,128,256]{3,2,1,0:T(8,128)(2,1)} %get-tuple-element.550, s32[1024]{0:T(1024)S(1)} %pad_clamp_fusion.4), kind=kCustom, calls=%fused_computation.4.clone.1 | custom fusion | bytes 2097184 | tf_op jit(solution)/shard_map/while/body/eval_jaxpr/jit(_take)/gather | solution.py:91
  42.0 6.4 %gather_fusion.2 = bf16[8,2,128,256]{3,2,1,0:T(8,128)(2,1)S(1)} fusion(bf16[2,128,128,256]{3,2,1,0:T(8,128)(2,1)} %get-tuple-element.550, s32[1024]{0:T(1024)S(1)} %pad_clamp_fusion.4), kind=kCustom, calls=%fused_computation.4.clone.1 | custom fusion | bytes 2097184 | tf_op jit(solution)/shard_map/while/body/eval_jaxpr/jit(_take)/gather | solution.py:91
  56.4 6.4 %gather_fusion.2 = bf16[8,2,128,256]{3,2,1,0:T(8,128)(2,1)S(1)} fusion(bf16[2,128,128,256]{3,2,1,0:T(8,128)(2,1)} %get-tuple-element.550, s32[1024]{0:T(1024)S(1)} %pad_clamp_fusion.4), kind=kCustom, calls=%fused_computation.4.clone.1 | custom fusion | bytes 2097184 | tf_op jit(solution)/shard_map/while/body/eval_jaxpr/jit(_take)/gather | solution.py:91
  70.8 6.4 %gather_fusion.2 = bf16[8,2,128,256]{3,2,1,0:T(8,128)(2,1)S(1)} fusion(bf16[2,128,128,256]{3,2,1,0:T(8,128)(2,1)} %get-tuple-element.550, s32[1024]{0:T(1024)S(1)} %pad_clamp_fusion.4), kind=kCustom, calls=%fused_computation.4.clone.1 | custom fusion | bytes 2097184 | tf_op jit(solution)/shard_map/while/body/eval_jaxpr/jit(_take)/gather | solution.py:91
  85.2 6.4 %gather_fusion.2 = bf16[8,2,128,256]{3,2,1,0:T(8,128)(2,1)S(1)} fusion(bf16[2,128,128,256]{3,2,1,0:T(8,128)(2,1)} %get-tuple-element.550, s32[1024]{0:T(1024)S(1)} %pad_clamp_fusion.4), kind=kCustom, calls=%fused_computation.4.clone.1 | custom fusion | bytes 2097184 | tf_op jit(solution)/shard_map/while/body/eval_jaxpr/jit(_take)/gather | solution.py:91
  99.5 6.4 %gather_fusion.2 = bf16[8,2,128,256]{3,2,1,0:T(8,128)(2,1)S(1)} fusion(bf16[2,128,128,256]{3,2,1,0:T(8,128)(2,1)} %get-tuple-element.550, s32[1024]{0:T(1024)S(1)} %pad_clamp_fusion.4), kind=kCustom, calls=%fused_computation.4.clone.1 | custom fusion | bytes 2097184 | tf_op jit(solution)/shard_map/while/body/eval_jaxpr/jit(_take)/gather | solution.py:91
  113.9 6.4 %gather_fusion.2 = bf16[8,2,128,256]{3,2,1,0:T(8,128)(2,1)S(1)} fusion(bf16[2,128,128,256]{3,2,1,0:T(8,128)(2,1)} %get-tuple-element.550, s32[1024]{0:T(1024)S(1)} %pad_clamp_fusion.4), kind=kCustom, calls=%fused_computation.4.clone.1 | custom fusion | bytes 2097184 | tf_op jit(solution)/shard_map/while/body/eval_jaxpr/jit(_take)/gather | solution.py:91
  128.3 6.4 %gather_fusion.2 = bf16[8,2,128,256]{3,2,1,0:T(8,128)(2,1)S(1)} fusion(bf16[2,128,128,256]{3,2,1,0:T(8,128)(2,1)} %get-tuple-element.550, s32[1024]{0:T(1024)S(1)} %pad_clamp_fusion.4), kind=kCustom, calls=%fused_computation.4.clone.1 | custom fusion | bytes 2097184 | tf_op jit(solution)/shard_map/while/body/eval_jaxpr/jit(_take)/gather | solution.py:91
  142.7 6.4 %gather_fusion.2 = bf16[8,2,128,256]{3,2,1,0:T(8,128)(2,1)S(1)} fusion(bf16[2,128,128,256]{3,2,1,0:T(8,128)(2,1)} %get-tuple-element.550, s32[1024]{0:T(1024)S(1)} %pad_clamp_fusion.4), kind=kCustom, calls=%fused_computation.4.clone.1 | custom fusion | bytes 2097184 | tf_op jit(solution)/shard_map/while/body/eval_jaxpr/jit(_take)/gather | solution.py:91
  157.0 6.4 %gather_fusion.2 = bf16[8,2,128,256]{3,2,1,0:T(8,128)(2,1)S(1)} fusion(bf16[2,128,128,256]{3,2,1,0:T(8,128)(2,1)} %get-tuple-element.550, s32[1024]{0:T(1024)S(1)} %pad_clamp_fusion.4), kind=kCustom, calls=%fused_computation.4.clone.1 | custom fusion | bytes 2097184 | tf_op jit(solution)/shard_map/while/body/eval_jaxpr/jit(_take)/gather | solution.py:91
  171.4 6.4 %gather_fusion.2 = bf16[8,2,128,256]{3,2,1,0:T(8,128)(2,1)S(1)} fusion(bf16[2,128,128,256]{3,2,1,0:T(8,128)(2,1)} %get-tuple-element.550, s32[1024]{0:T(1024)S(1)} %pad_clamp_fusion.4), kind=kCustom, calls=%fused_computation.4.clone.1 | custom fusion | bytes 2097184 | tf_op jit(solution)/shard_map/while/body/eval_jaxpr/jit(_take)/gather | solution.py:91
  185.8 6.4 %gather_fusion.2 = bf16[8,2,128,256]{3,2,1,0:T(8,128)(2,1)S(1)} fusion(bf16[2,128,128,256]{3,2,1,0:T(8,128)(2,1)} %get-tuple-element.550, s32[1024]{0:T(1024)S(1)} %pad_clamp_fusion.4), kind=kCustom, calls=%fused_computation.4.clone.1 | custom fusion | bytes 2097184 | tf_op jit(solution)/shard_map/while/body/eval_jaxpr/jit(_take)/gather | solution.py:91
  200.2 6.4 %gather_fusion.2 = bf16[8,2,128,256]{3,2,1,0:T(8,128)(2,1)S(1)} fusion(bf16[2,128,128,256]{3,2,1,0:T(8,128)(2,1)} %get-tuple-element.550, s32[1024]{0:T(1024)S(1)} %pad_clamp_fusion.4), kind=kCustom, calls=%fused_computation.4.clone.1 | custom fusion | bytes 2097184 | tf_op jit(solution)/shard_map/while/body/eval_jaxpr/jit(_take)/gather | solution.py:91
  214.6 6.4 %gather_fusion.2 = bf16[8,2,128,256]{3,2,1,0:T(8,128)(2,1)S(1)} fusion(bf16[2,128,128,256]{3,2,1,0:T(8,128)(2,1)} %get-tuple-element.550, s32[1024]{0:T(1024)S(1)} %pad_clamp_fusion.4), kind=kCustom, calls=%fused_computation.4.clone.1 | custom fusion | bytes 2097184 | tf_op jit(solution)/shard_map/while/body/eval_jaxpr/jit(_take)/gather | solution.py:91
  228.9 6.4 %gather_fusion.2 = bf16[8,2,128,256]{3,2,1,0:T(8,128)(2,1)S(1)} fusion(bf16[2,128,128,256]{3,2,1,0:T(8,128)(2,1)} %get-tuple-element.550, s32[1024]{0:T(1024)S(1)} %pad_clamp_fusion.4), kind=kCustom, calls=%fused_computation.4.clone.1 | custom fusion | bytes 2097184 | tf_op jit(solution)/shard_map/while/body/eval_jaxpr/jit(_take)/gather | solution.py:91
  255.6 9.7 %all-gather.1 = f32[1024,4]{0,1:T(4,128)S(1)} all-gather(f32[128,4]{0,1:T(4,128)S(1)} %get-tuple-element.248), channel_id=3, replica_groups=mesh['dp'=8,'mp'=4] {'dp'}, dimensions={0}, use_global_device_ids=true | all-gather | bytes 18432 | tf_op jit(solution)/shard_map/all_gather | solution.py:15
  265.3 7.9 %all-gather.2 = f32[1024,4]{0,1:T(4,128)S(1)} all-gather(f32[128,4]{0,1:T(4,128)S(1)} %get-tuple-element.249), channel_id=4, replica_groups=mesh['dp'=8,'mp'=4] {'dp'}, dimensions={0}, use_global_device_ids=true | all-gather | bytes 18432 | tf_op jit(solution)/shard_map/all_gather | solution.py:15
  273.2 7.2 %all-gather.6.cloned.1.call-done = f32[1024,4,64]{0,2,1:T(8,128)} async-done(((f32[128,4,64]{0,2,1:T(8,128)}), f32[1024,4,64]{0,2,1:T(8,128)}) %all-gather.6.cloned.1.call-update) | async-done | bytes 1048592 | tf_op jit(solution)/shard_map/all_gather | solution.py:15
  283.4 14.0 %while.33 = (s32[]{:T(128)}, f32[128,4]{0,1:T(4,128)S(1)}, f32[128,4]{0,1:T(4,128)S(1)}, f32[128,4,64]{2,1,0:T(4,128)S(1)}, f32[7,128,4]{1,2,0:T(4,128)S(1)}, /*...) while((s32[]{:T(128)}, f32[128,4]{0,1:T(4,128)S(1)}, f32[128,4]{0,1:T(4,128)S(1)}, ...), condition=%wide.region_8.9_spmd, body=%wide.region_7.8_spmd.sunk | while | flops 101378 | bytes 421989 | solution.py:18
  304.2 6.4 %copy.119 = bf16[2048,1024]{1,0:T(8,128)(2,1)} copy(bf16[2048,1024]{0,1:T(8,128)(2,1)} %bitcast.106) | data formatting | bytes 8388608 | tf_op jit(solution)/shard_map/dot_general | solution.py:144
  310.6 22.1 %all-reduce.3.cloned.1.call-done = f32[16,1024]{1,0:T(8,128)} async-done(((f32[16,1024]{1,0:T(8,128)}), f32[16,1024]{1,0:T(8,128)}) %all-reduce.3.cloned.1.call-update) | async-done | bytes 65552 | tf_op jit(solution)/shard_map/psum | solution.py:138
  338.7 33.2 %all-reduce.5.cloned.1.call-done = f32[16,1024]{1,0:T(8,128)} async-done(((f32[16,1024]{1,0:T(8,128)}), f32[16,1024]{1,0:T(8,128)}) %all-reduce.5.cloned.1.call-update) | async-done | bytes 65552 | tf_op jit(solution)/shard_map/psum | solution.py:150
  (577 shorter events, 171.6 us)
Async XLA Ops:
  7.2 329.9 %copy-start = (bf16[1024,1024]{1,0:T(8,128)(2,1)S(1)}, bf16[1024,1024]{1,0:T(8,128)(2,1)}, u32[]{:S(2)}) copy-start(bf16[1024,1024]{1,0:T(8,128)(2,1)} %param.21) | copy-start | bytes 6291460
  7.2 3.7 copy-start.6
  7.2 3.7 copy-start.7
  7.2 273.2 %all-gather.6.cloned.1.call-start = ((), (), s32[]{:S(2)}) async-start(), calls=%async_computation.2 | async-start | bytes 1179648 | tf_op jit(solution)/shard_map/all_gather | solution.py:15
  10.9 13.9 %copy-start.1 = (s32[128]{0:T(128)S(1)}, s32[128]{0:T(128)}, u32[]{:S(2)}) copy-start(s32[128]{0:T(128)} %param.24) | copy-start | bytes 1540
  10.9 13.9 %copy-start.2 = (s32[128]{0:T(128)S(1)}, s32[128]{0:T(128)}, u32[]{:S(2)}) copy-start(s32[128]{0:T(128)} %param.25) | copy-start | bytes 1540
  10.9 13.9 %copy-start.3 = (s32[128]{0:T(128)S(1)}, s32[128]{0:T(128)}, u32[]{:S(2)}) copy-start(s32[128]{0:T(128)} %param.23) | copy-start | bytes 1540
  254.9 0.6 copy-start.4
  255.5 77.2 %all-reduce.3.cloned.1.call-start = ((), (), s32[]{:S(2)}) async-start(), calls=%async_computation | async-start | bytes 131072 | tf_op jit(solution)/shard_map/psum | solution.py:138
  280.4 1.2 slice-start
  283.4 14.4 %copy-start.5 = (bf16[256,1024]{1,0:T(8,128)(2,1)S(1)}, bf16[256,1024]{1,0:T(8,128)(2,1)}, u32[]{:S(2)}) copy-start(bf16[256,1024]{1,0:T(8,128)(2,1)} %param.18) | copy-start | bytes 1572868
  298.6 73.4 %all-reduce.5.cloned.1.call-start = ((), (), s32[]{:S(2)}) async-start(), calls=%async_computation.1 | async-start | bytes 131072 | tf_op jit(solution)/shard_map/psum | solution.py:150
  304.2 29.5 %copy-start.8 = (f32[1024]{0:T(1024)S(1)}, f32[1024]{0:T(1024)}, u32[]{:S(2)}) copy-start(f32[1024]{0:T(1024)} %param.19) | copy-start | bytes 12292
Sparse Core Ops, SparseCore 0:
  255.7 24.6 all-gather.5
  298.7 33.9 all-reduce.2
  338.2 33.6 all-reduce.4
where the time goes:
time: 382 us; the launch traced here: 380 us
  local copies, waits for them, and re-layouts  201 us (53%)
  waiting for transfers between devices  62.5 us (16%)
  matrix products  43.1 us (11%)
  other arithmetic  29.2 us (8%)
  blocking collectives  28.3 us (7%)
  between operations  14 us (4%)
    gather x16, local copies, waits for them, and re-layouts, visit(): fetched = jnp.take(kv_cache, picked, axis=1)  102 us
    psum x1, waiting for transfers between devices, body(): lax.psum(jnp.dot(activated, w_down, preferred_element_type=jnp.float32),...  33.2 us
    psum x1, waiting for transfers between devices, body(): lax.psum(jnp.dot(context, w_out, preferred_element_type=jnp.float32), 'mp')  22.1 us
    dot_general x16, matrix products, visit(): jnp.einsum('phd,pthd->pht', chosen_queries, key_rows, preferred_element_t...  20.4 us
    all_gather x2, blocking collectives, merged_2(): pieces = jax.tree.map(lambda part: lax.all_gather(part, axis), value)  17.6 us
    slice x16, local copies, waits for them, and re-layouts, visit(): key_rows = fetched[0].reshape(PAGE_BLOCK, page_len, local_heads, HEAD_DIM)  15.9 us
    add x7, other arithmetic, combine(): first[2] * shrink_first[:, :, None] + second[2] * shrink_second[:, :, None]  12.2 us
    all_gather x1, blocking collectives, body(): every_query = lax.all_gather(projected[:, 0], 'dp', axis=0, tiled=True)  10.7 us
  transfers between devices with their start and end apart: 3, of which 3 were waited for; matrix products, arithmetic and copies ran while one was open for 3% of the time, Pallas kernels for 0%

commit v1 on v0

v1 whole, which is shorter than its diff:
```python
import functools

import jax
import jax.numpy as jnp
from jax import lax
from jax.experimental import pallas as pl
from jax.experimental.pallas import tpu as pltpu
from jax.sharding import PartitionSpec as P

HEAD_DIM = 64
CHUNK = 8
LANES = 128
EPSILON = 1e-05
NEGATIVE = -1e30
F32 = jnp.float32
BF16 = jnp.bfloat16


def rms_norm(values, gain):
    widened = values.astype(F32)
    mean_square = jnp.mean(widened * widened, axis=-1, keepdims=True)
    return (widened * lax.rsqrt(mean_square + EPSILON) * gain).astype(BF16)


def dot(a, b):
    return jnp.dot(a, b, preferred_element_type=F32)


def kernel(
    n_dp,
    n_mp,
    hidden,
    attn_gain,
    w_qkv_hbm,
    w_out_hbm,
    mlp_gain,
    w_gu_hbm,
    w_down_hbm,
    kv_hbm,
    lengths,
    owners,
    places,
    appended,
    hidden_out,
    w_qkv,
    w_out,
    w_gu,
    w_down,
    kv,
    queries,
    partial_out,
    partial_in,
    sums_one,
    sums_two,
    page_query,
    bias,
    page_stats,
    page_sum,
    w_sem,
    kv_sem,
    q_send,
    q_recv,
    p_send,
    p_recv,
    s_send,
    s_recv,
):
    rows, width = hidden.shape
    cols = w_qkv.shape[2]
    heads = cols // HEAD_DIM
    pages, page_len = kv.shape[1], kv.shape[2]
    requests = rows * n_dp
    chunks = pages // CHUNK
    me_dp = lax.axis_index("dp")
    me_mp = lax.axis_index("mp")

    w_copies = [
        pltpu.make_async_copy(src, dst, w_sem.at[i])
        for i, (src, dst) in enumerate(
            ((w_qkv_hbm, w_qkv), (w_out_hbm, w_out), (w_gu_hbm, w_gu), (w_down_hbm, w_down))
        )
    ]
    w_copies[0].start()

    def kv_copy(c):
        at = pl.ds(c * CHUNK, CHUNK)
        return pltpu.make_async_copy(kv_hbm.at[:, at], kv.at[:, at], kv_sem.at[c])

    barrier = pltpu.get_barrier_semaphore()
    for k in range(1, n_dp):
        pl.semaphore_signal(
            barrier,
            inc=1,
            device_id=(lax.rem(me_dp + k, n_dp), me_mp),
            device_id_type=pl.DeviceIdType.MESH,
        )
    for k in range(1, n_mp):
        pl.semaphore_signal(
            barrier,
            inc=1,
            device_id=(me_dp, lax.rem(me_mp + k, n_mp)),
            device_id_type=pl.DeviceIdType.MESH,
        )
    lax.fori_loop(0, chunks, lambda c, _: kv_copy(c).start(), None)
    for copy in w_copies[1:]:
        copy.start()

    normed = rms_norm(hidden[...], attn_gain[...])
    w_copies[0].wait()
    own_query, own_key, own_value = (dot(normed, w_qkv[i]).astype(BF16) for i in range(3))
    appended[0] = own_key
    appended[1] = own_value
    queries[me_dp] = own_query
    pl.semaphore_wait(barrier, n_dp + n_mp - 2)

    def query_copy(k, slot):
        return pltpu.make_async_remote_copy(
            src_ref=queries.at[slot],
            dst_ref=queries.at[slot],
            send_sem=q_send.at[k],
            recv_sem=q_recv.at[k],
            device_id=(lax.rem(me_dp + k, n_dp), me_mp),
            device_id_type=pl.DeviceIdType.MESH,
        )

    for k in range(1, n_dp):
        query_copy(k, me_dp).start()

    owner_row = owners[...]
    owner_by_request = jnp.broadcast_to(owner_row, (requests, pages))
    member_rp = owner_by_request == lax.broadcasted_iota(jnp.int32, (requests, pages), 0)
    owner_by_page = jnp.transpose(owner_by_request.astype(F32))
    member_pr = owner_by_page == lax.broadcasted_iota(jnp.int32, (pages, requests), 1).astype(F32)
    page_length = jnp.sum(jnp.where(member_pr, lengths[...].astype(F32), 0.0), axis=1, keepdims=True)
    place = jnp.transpose(jnp.broadcast_to(places[...], (page_len, pages)).astype(F32))
    token = lax.broadcasted_iota(jnp.int32, (pages, page_len), 1).astype(F32)
    bias[...] = jnp.where(place * page_len + token < page_length, 0.0, NEGATIVE)

    lane = lax.broadcasted_iota(jnp.int32, (rows, LANES), 1)
    product = own_query.astype(F32) * own_key.astype(F32)
    self_lse = jnp.full((rows, LANES), NEGATIVE, F32)
    for h in range(heads):
        score = jnp.sum(product[:, h * HEAD_DIM : (h + 1) * HEAD_DIM], axis=1, keepdims=True)
        self_lse = jnp.where(lane == h, score * HEAD_DIM**-0.5, self_lse)

    for k in range(1, n_dp):
        query_copy(k, lax.rem(me_dp + n_dp - k, n_dp)).wait_recv()
    every_query = queries[...].reshape(requests, cols)
    page_query[...] = dot(member_pr.astype(F32).astype(BF16), every_query) * HEAD_DIM**-0.5

    head_mask = (
        lax.broadcasted_iota(jnp.int32, (8, cols), 1) // HEAD_DIM
        == lax.broadcasted_iota(jnp.int32, (8, cols), 0)
    ).astype(F32)
    half = lax.broadcasted_iota(jnp.int32, (8, LANES), 1) < LANES // 2

    def visit(c, _):
        kv_copy(c).wait()
        for j in range(CHUNK):
            p = c * CHUNK + j
            query = (page_query[pl.ds(p, 1), :] * head_mask).astype(BF16)
            dead = bias[pl.ds(p, 1), :]
            scores = (
                lax.dot_general(
                    query, kv[0, p], (((1,), (1,)), ((), ())), preferred_element_type=F32
                )
                + dead
            )
            largest = jnp.max(scores, axis=1, keepdims=True)
            raw = jnp.where(dead < 0.0, 0.0, jnp.exp(scores - largest))
            total = jnp.sum(raw, axis=1, keepdims=True)
            page_stats[p] = jnp.where(half, largest, total)
            values = dot(raw.astype(BF16), kv[1, p]) * head_mask
            page_sum[pl.ds(p, 1), :] = jnp.sum(values, axis=0, keepdims=True)
        return None

    lax.fori_loop(0, chunks, visit, None)

    part = lax.broadcasted_iota(jnp.int32, (requests, cols), 1) // HEAD_DIM
    stat_lane = lax.broadcasted_iota(jnp.int32, (requests, LANES), 1)
    factor_part = lax.broadcasted_iota(jnp.int32, (cols, pages), 0) // HEAD_DIM
    factors = jnp.zeros((cols, pages), F32)
    inverse = jnp.zeros((requests, cols), F32)
    lse = jnp.full((requests, LANES), NEGATIVE, F32)
    for h in range(heads):
        stats = jnp.transpose(page_stats[:, h, :])
        max_row = stats[0:1, :]
        total_row = stats[LANES // 2 : LANES // 2 + 1, :]
        top = jnp.max(jnp.where(member_rp, max_row, NEGATIVE), axis=1, keepdims=True)
        top_row = jnp.sum(jnp.where(member_rp, top, 0.0), axis=0, keepdims=True)
        factor = jnp.where(owner_row >= 0, jnp.exp(jnp.minimum(max_row - top_row, 0.0)), 0.0)
        total = jnp.sum(jnp.where(member_rp, factor * total_row, 0.0), axis=1, keepdims=True)
        filled = total > 0.0
        safe = jnp.where(filled, total, 1.0)
        factors = jnp.where(factor_part == h, factor, factors)
        inverse = jnp.where(part == h, 1.0 / safe, inverse)
        lse = jnp.where(
            stat_lane == h, jnp.where(filled, top + jnp.log(safe), NEGATIVE), lse
        )
    scaled = page_sum[...] * jnp.transpose(factors)
    high = scaled.astype(BF16)
    low = (scaled - high.astype(F32)).astype(BF16)
    member = member_rp.astype(F32).astype(BF16)
    local = (dot(member, high) + dot(member, low)) * inverse
    partial_out[:, :, 0:cols] = local.reshape(n_dp, rows, cols)
    partial_out[:, :, cols : cols + LANES] = lse.reshape(n_dp, rows, LANES)

    def partial_copy(k):
        to = lax.rem(me_dp + k, n_dp)
        return pltpu.make_async_remote_copy(
            src_ref=partial_out.at[to],
            dst_ref=partial_in.at[k],
            send_sem=p_send.at[k],
            recv_sem=p_recv.at[k],
            device_id=(to, me_mp),
            device_id_type=pl.DeviceIdType.MESH,
        )

    for k in range(1, n_dp):
        partial_copy(k).start()
    partial_in[0] = partial_out[me_dp]
    for k in range(1, n_dp):
        partial_copy(k).wait_recv()

    lses = partial_in[:, :, cols : cols + LANES]
    top = jnp.maximum(self_lse, jnp.max(lses, axis=0))
    self_share = jnp.exp(self_lse - top)
    shares = jnp.exp(lses - top[None])
    total = self_share + jnp.sum(shares, axis=0)
    column = lax.broadcasted_iota(jnp.int32, (rows, cols), 1) // HEAD_DIM

    def widen(share):
        wide = jnp.zeros((rows, cols), F32)
        for h in range(heads):
            wide = jnp.where(column == h, share[:, h : h + 1], wide)
        return wide

    weighted = widen(self_share) * own_value.astype(F32)
    for k in range(n_dp):
        weighted = weighted + widen(shares[k]) * partial_in[k, :, 0:cols]
    context = (weighted / widen(total)).astype(BF16)

    def sum_over_mp(term, slots, at):
        slots[me_mp] = term.astype(BF16)

        def copy(k, slot):
            return pltpu.make_async_remote_copy(
                src_ref=slots.at[slot],
                dst_ref=slots.at[slot],
                send_sem=s_send.at[at, k],
                recv_sem=s_recv.at[at, k],
                device_id=(me_dp, lax.rem(me_mp + k, n_mp)),
                device_id_type=pl.DeviceIdType.MESH,
            )

        for k in range(1, n_mp):
            copy(k, me_mp).start()
        for k in range(1, n_mp):
            copy(k, lax.rem(me_mp + n_mp - k, n_mp)).wait_recv()
        for k in range(1, n_mp):
            copy(k, me_mp).wait_send()
        return jnp.sum(slots[...].astype(F32), axis=0)

    w_copies[1].wait()
    attended = sum_over_mp(dot(context, w_out[...]), sums_one, 0)
    residual = (hidden[...].astype(F32) + attended).astype(BF16)
    normed_mlp = rms_norm(residual, mlp_gain[...])

    tiles = width // LANES
    spread_from = lax.broadcasted_iota(jnp.int32, (LANES, 4 * LANES), 0)
    spread_to = lax.broadcasted_iota(jnp.int32, (LANES, 4 * LANES), 1)
    even = spread_to == 2 * spread_from
    odd = spread_to == 2 * LANES + 2 * spread_from + 1
    spread = (even | odd).astype(F32).astype(BF16)
    stacked = jnp.concatenate(
        [normed_mlp[:, i * LANES : (i + 1) * LANES] for i in range(tiles)], axis=0
    )
    apart = dot(stacked, spread).astype(BF16)
    w_copies[2].wait()
    gate_up = None
    for i in range(tiles):
        rows_i = apart[i * rows : (i + 1) * rows]
        left = jnp.concatenate([rows_i[:, : 2 * LANES], rows_i[:, 2 * LANES :]], axis=0)
        right = w_gu[i * LANES : (i + 1) * LANES].reshape(2 * LANES, w_gu.shape[2])
        step = dot(left, right)
        gate_up = step if gate_up is None else gate_up + step
    gate, up = gate_up[:rows], gate_up[rows:]
    activated = (gate / (1.0 + jnp.exp(-gate)) * up).astype(BF16)
    w_copies[3].wait()
    lowered = sum_over_mp(dot(activated, w_down[...]), sums_two, 1)
    hidden_out[...] = (residual.astype(F32) + lowered).astype(BF16)

    for k in range(1, n_dp):
        query_copy(k, me_dp).wait_send()
        partial_copy(k).wait_send()


def body(n_dp, n_mp, hidden, attn_gain, w_qkv, w_out, mlp_gain, w_gate_up, w_down, kv_cache, lengths, page_request, page_index):
    rows, width = hidden.shape
    cols = w_qkv.shape[2]
    pages, page_len = kv_cache.shape[1:3]
    vmem = pl.BlockSpec(memory_space=pltpu.VMEM)
    hbm = pl.BlockSpec(memory_space=pl.ANY)
    dma = pltpu.SemaphoreType.DMA
    w_qkv = jnp.transpose(w_qkv, (1, 0, 2))
    return pl.pallas_call(
        functools.partial(kernel, n_dp, n_mp),
        out_shape=(
            jax.ShapeDtypeStruct((2, rows, cols), BF16),
            jax.ShapeDtypeStruct((rows, width), BF16),
        ),
        in_specs=[vmem, vmem, hbm, hbm, vmem, hbm, hbm, hbm, vmem, vmem, vmem],
        out_specs=(vmem, vmem),
        scratch_shapes=[
            pltpu.VMEM(w_qkv.shape, BF16),
            pltpu.VMEM(w_out.shape, BF16),
            pltpu.VMEM(w_gate_up.shape, BF16),
            pltpu.VMEM(w_down.shape, BF16),
            pltpu.VMEM(kv_cache.shape, BF16),
            pltpu.VMEM((n_dp, rows, cols), BF16),
            pltpu.VMEM((n_dp, rows, cols + LANES), F32),
            pltpu.VMEM((n_dp, rows, cols + LANES), F32),
            pltpu.VMEM((n_mp, rows, width), BF16),
            pltpu.VMEM((n_mp, rows, width), BF16),
            pltpu.VMEM((pages, cols), F32),
            pltpu.VMEM((pages, page_len), F32),
            pltpu.VMEM((pages, 8, LANES), F32),
            pltpu.VMEM((pages, cols), F32),
            dma((4,)),
            dma((pages // CHUNK,)),
            dma((n_dp,)),
            dma((n_dp,)),
            dma((n_dp,)),
            dma((n_dp,)),
            dma((2, n_mp)),
            dma((2, n_mp)),
        ],
        compiler_params=pltpu.CompilerParams(
            collective_id=0, has_side_effects=True, vmem_limit_bytes=56 * 1024 * 1024
        ),
    )(
        hidden,
        attn_gain.reshape(1, width),
        w_qkv,
        w_out,
        mlp_gain.reshape(1, width),
        w_gate_up,
        w_down,
        kv_cache,
        lengths.reshape(1, -1),
        page_request.reshape(1, -1),
        page_index.reshape(1, -1),
    )


def solution(mesh):
    return jax.shard_map(
        functools.partial(body, mesh.shape["dp"], mesh.shape["mp"]),
        mesh=mesh,
        in_specs=(
            P("dp", None),
            P(),
            P(None, None, "mp"),
            P("mp", None),
            P(),
            P(None, None, "mp"),
            P("mp", None),
            P(None, "dp", None, "mp"),
            P(),
            P("dp"),
            P("dp"),
        ),
        out_specs=(P(None, "dp", "mp"), P("dp", None)),
        check_vma=False,
    )
```

time: 382 us -> 61.7 us (0.16)
  local copies, waits for them, and re-layouts: 201 us -> 2.7 us
  waiting for transfers between devices: 62.5 us -> 0 us
  Pallas kernels: 0 us -> 58 us
  matrix products: 43.1 us -> 0 us
  other arithmetic: 29.2 us -> 0 us
  blocking collectives: 28.3 us -> 0 us
  between operations: 14 us -> 0.64 us
    gather x96 -> x0, local copies, waits for them, and re-layouts: 151 us -> none  [the longest x16 102 us: visit(): fetched = jnp.take(kv_cache, picked, axis=1)]
    pallas_call x0 -> x1, Pallas kernels: none -> 58 us  [body(): pl.pallas_call(functools.partial(kernel, n_dp, n_mp), out_shape=(jax.Shap...]
    psum x2 -> x0, waiting for transfers between devices: 55.3 us -> none  [the longest x1 33.2 us: body(): lax.psum(jnp.dot(activated, w_down, preferred_element_type=jnp.float32),...]
    dot_general x68 -> x0, matrix products: 43.1 us -> none  [the longest x16 20.4 us: visit(): jnp.einsum('phd,pthd->pht', chosen_queries, key_rows, preferred_element_t...]
    all_gather x3 -> x0, blocking collectives: 28.3 us -> none  [the longest x2 17.6 us: merged_2(): pieces = jax.tree.map(lambda part: lax.all_gather(part, axis), value)]
    slice x54 -> x0, local copies, waits for them, and re-layouts: 23 us -> none  [the longest x16 15.9 us: visit(): key_rows = fetched[0].reshape(PAGE_BLOCK, page_len, local_heads, HEAD_DIM)]
    add x14 -> x0, other arithmetic: 12.4 us -> none  [the longest x7 12.2 us: combine(): first[2] * shrink_first[:, :, None] + second[2] * shrink_second[:, :, None]]
    all_gather x1 -> x0, waiting for transfers between devices: 7.19 us -> none  [merged_2(): pieces = jax.tree.map(lambda part: lax.all_gather(part, axis), value)]
  transfers between devices with their start and end apart: 3 -> 0, of which waited for: 3 -> 0; matrix products, arithmetic and copies ran while one was open for 3% -> 0% of each run, Pallas kernels for 0% -> 0%
where the time goes in v1:
time: 61.7 us; the launch traced here: 61.4 us
  Pallas kernels  58 us (94%)
  local copies, waits for them, and re-layouts  2.7 us (4%)
  between operations  0.64 us (1%)
    pallas_call x1, Pallas kernels, body(): pl.pallas_call(functools.partial(kernel, n_dp, n_mp), out_shape=(jax.Shap...  58 us
    unnamed x2, local copies, waits for them, and re-layouts  2.7 us

profile of v1, /device:TPU:0, one launch (start us, length us, event | category | flops | bytes accessed | tf_op | source)
XLA Modules:
  0.0 61.4 jit_solution(1795342711111862255)
XLA Ops:
  0.6 58.0 %shard_map.122 = (bf16[2,16,256]{2,1,0:T(8,128)(2,1)}, bf16[16,1024]{1,0:T(8,128)(2,1)}) custom-call(bf16[16,1024]{1,0:T(8,128)(2,1)} %hidden.1, f32[1,1024]{1,0:T(1,128)} %bitcast.7, bf16[3,1024,256]{2,1,0:T(8,128)(2,1)} %bitcast.6, bf16[256,1024]{1,0:T(8,128)(2,1)} %w_out_hbm.1, f32[1,1024]{1,0:T(1,128)} %bitcast.8, bf16[1024,2,1024]{2,1,0:T(2,128)(2,1)} %w_gu_hbm.1, ...), custom_call_target="tpu_custom_call" | custom-call | tf_op jit(solution)/shard_map/pallas_call | solution.py:306
  58.7 1.3 %copy.15 = bf16[2,16,256]{2,1,0:T(8,128)(2,1)} copy(bf16[2,16,256]{2,1,0:T(8,128)(2,1)} %get-tuple-element.4) | data formatting | bytes 32768
  60.0 1.4 %copy.16 = bf16[16,1024]{1,0:T(8,128)(2,1)} copy(bf16[16,1024]{1,0:T(8,128)(2,1)} %get-tuple-element.5) | data formatting | bytes 65536

commit v2 on v1

--- a/solution.py
+++ b/solution.py
@@ -152,26 +152,44 @@
         lax.broadcasted_iota(jnp.int32, (8, cols), 1) // HEAD_DIM
         == lax.broadcasted_iota(jnp.int32, (8, cols), 0)
     ).astype(F32)
-    half = lax.broadcasted_iota(jnp.int32, (8, LANES), 1) < LANES // 2
+    half = lax.broadcasted_iota(jnp.int32, (8 * CHUNK, LANES), 1) < LANES // 2
 
     def visit(c, _):
         kv_copy(c).wait()
-        for j in range(CHUNK):
-            p = c * CHUNK + j
-            query = (page_query[pl.ds(p, 1), :] * head_mask).astype(BF16)
-            dead = bias[pl.ds(p, 1), :]
-            scores = (
+        at = pl.ds(c * CHUNK, CHUNK)
+        chunk_query = page_query[at, :]
+        chunk_bias = bias[at, :]
+        dead = jnp.concatenate(
+            [jnp.broadcast_to(chunk_bias[j : j + 1], (8, page_len)) for j in range(CHUNK)], axis=0
+        )
+        scores = jnp.concatenate(
+            [
                 lax.dot_general(
-                    query, kv[0, p], (((1,), (1,)), ((), ())), preferred_element_type=F32
+                    (chunk_query[j : j + 1] * head_mask).astype(BF16),
+                    kv[0, c * CHUNK + j],
+                    (((1,), (1,)), ((), ())),
+                    preferred_element_type=F32,
                 )
-                + dead
-            )
-            largest = jnp.max(scores, axis=1, keepdims=True)
-            raw = jnp.where(dead < 0.0, 0.0, jnp.exp(scores - largest))
-            total = jnp.sum(raw, axis=1, keepdims=True)
-            page_stats[p] = jnp.where(half, largest, total)
-            values = dot(raw.astype(BF16), kv[1, p]) * head_mask
-            page_sum[pl.ds(p, 1), :] = jnp.sum(values, axis=0, keepdims=True)
+                for j in range(CHUNK)
+            ],
+            axis=0,
+        ) + dead
+        largest = jnp.max(scores, axis=1, keepdims=True)
+        raw = jnp.where(dead < 0.0, 0.0, jnp.exp(scores - largest))
+        total = jnp.sum(raw, axis=1, keepdims=True)
+        page_stats[at] = jnp.where(half, largest, total).reshape(CHUNK, 8, LANES)
+        weights = raw.astype(BF16)
+        page_sum[at, :] = jnp.concatenate(
+            [
+                jnp.sum(
+                    dot(weights[8 * j : 8 * j + 8], kv[1, c * CHUNK + j]) * head_mask,
+                    axis=0,
+                    keepdims=True,
+                )
+                for j in range(CHUNK)
+            ],
+            axis=0,
+        )
         return None
 
     lax.fori_loop(0, chunks, visit, None)

time: 61.7 us -> 37.4 us (0.61)
  Pallas kernels: 58 us -> 33.7 us
    pallas_call x1, Pallas kernels: 58 us -> 33.7 us  [body(): pl.pallas_call(functools.partial(kernel, n_dp, n_mp), out_shape=(jax.Shap...]
where the time goes in v2:
time: 37.4 us; the launch traced here: 37.1 us
  Pallas kernels  33.7 us (90%)
  local copies, waits for them, and re-layouts  2.7 us (7%)
  between operations  0.64 us (2%)
    pallas_call x1, Pallas kernels, body(): pl.pallas_call(functools.partial(kernel, n_dp, n_mp), out_shape=(jax.Shap...  33.7 us
    unnamed x2, local copies, waits for them, and re-layouts  2.7 us

profile of v2, /device:TPU:0, one launch (start us, length us, event | category | flops | bytes accessed | tf_op | source)
XLA Modules:
  0.0 37.1 jit_solution(15146710205558269456)
XLA Ops:
  0.6 33.7 %shard_map.122 = (bf16[2,16,256]{2,1,0:T(8,128)(2,1)}, bf16[16,1024]{1,0:T(8,128)(2,1)}) custom-call(bf16[16,1024]{1,0:T(8,128)(2,1)} %hidden.1, f32[1,1024]{1,0:T(1,128)} %bitcast.7, bf16[3,1024,256]{2,1,0:T(8,128)(2,1)} %bitcast.6, bf16[256,1024]{1,0:T(8,128)(2,1)} %w_out_hbm.1, f32[1,1024]{1,0:T(1,128)} %bitcast.8, bf16[1024,2,1024]{2,1,0:T(2,128)(2,1)} %w_gu_hbm.1, ...), custom_call_target="tpu_custom_call" | custom-call | tf_op jit(solution)/shard_map/pallas_call | solution.py:324
  34.4 1.3 %copy.15 = bf16[2,16,256]{2,1,0:T(8,128)(2,1)} copy(bf16[2,16,256]{2,1,0:T(8,128)(2,1)} %get-tuple-element.4) | data formatting | bytes 32768
  35.7 1.4 %copy.16 = bf16[16,1024]{1,0:T(8,128)(2,1)} copy(bf16[16,1024]{1,0:T(8,128)(2,1)} %get-tuple-element.5) | data formatting | bytes 65536

commit v3 on v2

--- a/solution.py
+++ b/solution.py
@@ -8,7 +8,7 @@
 from jax.sharding import PartitionSpec as P
 
 HEAD_DIM = 64
-CHUNK = 8
+CHUNK = 16
 LANES = 128
 EPSILON = 1e-05
 NEGATIVE = -1e30

time: 37.4 us -> 34.7 us (0.928)
  Pallas kernels: 33.7 us -> 31.1 us
    pallas_call x1, Pallas kernels: 33.7 us -> 31.1 us  [body(): pl.pallas_call(functools.partial(kernel, n_dp, n_mp), out_shape=(jax.Shap...]
where the time goes in v3:
time: 34.7 us; the launch traced here: 34.4 us
  Pallas kernels  31.1 us (90%)
  local copies, waits for them, and re-layouts  2.7 us (8%)
  between operations  0.64 us (2%)
    pallas_call x1, Pallas kernels, body(): pl.pallas_call(functools.partial(kernel, n_dp, n_mp), out_shape=(jax.Shap...  31.1 us
    unnamed x2, local copies, waits for them, and re-layouts  2.7 us

profile of v3, /device:TPU:0, one launch (start us, length us, event | category | flops | bytes accessed | tf_op | source)
XLA Modules:
  0.0 34.4 jit_solution(12623010546855973704)
XLA Ops:
  0.6 31.1 %shard_map.122 = (bf16[2,16,256]{2,1,0:T(8,128)(2,1)}, bf16[16,1024]{1,0:T(8,128)(2,1)}) custom-call(bf16[16,1024]{1,0:T(8,128)(2,1)} %hidden.1, f32[1,1024]{1,0:T(1,128)} %bitcast.7, bf16[3,1024,256]{2,1,0:T(8,128)(2,1)} %bitcast.6, bf16[256,1024]{1,0:T(8,128)(2,1)} %w_out_hbm.1, f32[1,1024]{1,0:T(1,128)} %bitcast.8, bf16[1024,2,1024]{2,1,0:T(2,128)(2,1)} %w_gu_hbm.1, ...), custom_call_target="tpu_custom_call" | custom-call | tf_op jit(solution)/shard_map/pallas_call | solution.py:324
  31.7 1.3 %copy.15 = bf16[2,16,256]{2,1,0:T(8,128)(2,1)} copy(bf16[2,16,256]{2,1,0:T(8,128)(2,1)} %get-tuple-element.4) | data formatting | bytes 32768
  33.0 1.4 %copy.16 = bf16[16,1024]{1,0:T(8,128)(2,1)} copy(bf16[16,1024]{1,0:T(8,128)(2,1)} %get-tuple-element.5) | data formatting | bytes 65536
